TPU v7x, 32 devices: a whole 2x2x4 slice. The times are simulated.
32 devices in a mesh: dp: 16 (over z, y, x), head: 2 (over core).
Axes of the slice: x: 2, y: 2, z: 4, core: 2. Of those that a mesh axis runs over, the one named last changes fastest.
Arguments:
- tokens: bfloat16 [288, 198, 384], P(('dp', 'head')), may hold values from -6 to 6
- cotangent: bfloat16 [288, 198, 384], P(('dp', 'head')), may hold values from -6 to 6
- keep_mask: int32 [288, 198], P(('dp', 'head')), may hold values from 0 to 1, as said below
- source: int32 [288], P(('dp', 'head')), may hold values from 0 to 95, as said below
- qkv_master: float32 [384, 1152], P('dp'), may hold values from -0.3125 to 0.3125
- proj_master: float32 [384, 384], P('dp'), may hold values from -1.25 to 1.25
- fc1_master: float32 [384, 1536], P('dp'), may hold values from -0.3125 to 0.3125
- fc2_master: float32 [1536, 384], P('dp'), may hold values from -0.15625 to 0.15625
- vec_master: float32 [12, 384], P(None, 'dp'), may hold values from -1.2 to 1.4, as said below
- qkv_first: float32 [384, 1152], P('dp'), may hold values from -160 to 160
- proj_first: float32 [384, 384], P('dp'), may hold values from -24 to 24
- fc1_first: float32 [384, 1536], P('dp'), may hold values from -40 to 40
- fc2_first: float32 [1536, 384], P('dp'), may hold values from -80 to 80
- vec_first: float32 [12, 384], P(None, 'dp'), may hold values from -160 to 160
- qkv_second: float32 [384, 1152], P('dp'), may hold values from 28.512 to 456.192
- proj_second: float32 [384, 384], P('dp'), may hold values from 0.6443712 to 10.26432
- fc1_second: float32 [384, 1536], P('dp'), may hold values from 1.7848512 to 28.512
- fc2_second: float32 [1536, 384], P('dp'), may hold values from 7.128 to 114.048
- vec_second: float32 [12, 384], P(None, 'dp'), may hold values from 28.512 to 456.192
Outputs:
- layer_out: bfloat16 [288, 198, 384], P(('dp', 'head'))
- input_grad: float32 [288, 198, 384], P(('dp', 'head'))
- qkv_first_new: float32 [384, 1152], P('dp')
- qkv_second_new: float32 [384, 1152], P('dp')
- qkv_new: float32 [384, 1152], P('dp')
- proj_first_new: float32 [384, 384], P('dp')
- proj_second_new: float32 [384, 384], P('dp')
- proj_new: float32 [384, 384], P('dp')
- fc1_first_new: float32 [384, 1536], P('dp')
- fc1_second_new: float32 [384, 1536], P('dp')
- fc1_new: float32 [384, 1536], P('dp')
- fc2_first_new: float32 [1536, 384], P('dp')
- fc2_second_new: float32 [1536, 384], P('dp')
- fc2_new: float32 [1536, 384], P('dp')
- vec_first_new: float32 [12, 384], P(None, 'dp')
- vec_second_new: float32 [12, 384], P(None, 'dp')
- vec_new: float32 [12, 384], P(None, 'dp')
Inputs may be any that keep to these rules, and one draw needn't show every extreme that they name: `keep_mask`: 1 keeps a token; tokens 0 and 1 of every image (class and distillation tokens) are always kept. Every source number names exactly three images, and these stand on three different indices of dp. `vec_master`: rows 0 and 5 lie between 0.6 and 1.4.
All inputs are finite; a program needn't handle non-finite values.
Results may differ from a plain program's by a relative error of at most 0.012.
The roundings to bfloat16 on the way count: a program that leaves them out, or rounds other values in their place, can miss the bound.
Values may be sent and summed in bfloat16 or wider, within the bound.
A program may use at most 128 MiB of HBM per device.

v0:
```python
import functools

import jax
import jax.numpy as jnp
from jax import lax
from jax.experimental import pallas as pl
from jax.experimental.pallas import tpu as pltpu
from jax.sharding import PartitionSpec as P

HEADS = 6
HEAD_DIM = 64
STEP = 10
PAIRS = HEADS // 2
SCALE = HEAD_DIM ** (-0.5)

norm_eps = 1e-06
step_rates = (0.1, 0.4, 0.1, 0.05, 0.5)
decays = (0.05, 0.05, 0.05, 0.05, 0.0)

UNITS = 12
PLANE = 4
SHARD = 24

ROW_PROJ, ROW_FC2, ROW_FC1, SUM_ROWS = 3, 4, 5, 16

F32 = jnp.float32
BF16 = jnp.bfloat16


def dot(left, right):
    return lax.dot_general(left, right, (((1,), (0,)), ((), ())), preferred_element_type=F32)


def across(left, right):
    return lax.dot_general(left, right, (((0,), (0,)), ((), ())), preferred_element_type=F32)


def against(left, right):
    return lax.dot_general(left, right, (((1,), (1,)), ((), ())), preferred_element_type=F32)


def normalise(values):
    average = jnp.mean(values, -1, keepdims=True)
    centred = values - average
    variance = jnp.mean(centred * centred, -1, keepdims=True)
    inverse = lax.rsqrt(variance + norm_eps)
    return centred * inverse, inverse


def norm_back(grad, unit, inverse, gain_row):
    scaled = grad * gain_row
    first = jnp.mean(scaled, -1, keepdims=True)
    second = jnp.mean(scaled * unit, -1, keepdims=True)
    return inverse * (scaled - first - unit * second)


def fold(values):
    rows, cols = values.shape
    return jnp.sum(values.reshape(rows // 8, 8, cols), 0)


LOG2E_HALF = 0.7213475204444817
INV_SQRT_2PI = 0.3989422804014327


def gelu_parts(x):
    cdf = 0.5 + 0.5 * lax.erf(x * 0.7071067811865476)
    bell = jnp.exp2(x * x * (-LOG2E_HALF)) * INV_SQRT_2PI
    return x * cdf, cdf + x * bell


def layer_kernel(linked, dp, sources, *refs):
    refs = list(refs)

    def take(count):
        taken = refs[:count]
        del refs[:count]
        return taken

    tok_hbm, cot_hbm, keep_ref = take(3)
    if linked:
        src_ref, qm_ref, pm_ref, f1_ref, f2_ref, vm_ref = take(6)
        out_hbm, gin_hbm, share_ref, vsum_ref = take(4)
        wq_ref, wp_ref, w1_ref, w2_ref, vec_ref = take(5)
        slabs, vslabs, tot_mine, tot_in, pair_in, plane_in, layer_out, layer_in, layer_in2 = take(9)
        vsum, vin, share_in, send, recv = take(5)
    else:
        tw_ref, wq_ref, wp_ref, w1_ref, w2_ref, vec_ref = take(6)
        out_hbm, gin_hbm, gq_ref, gp_ref, g1_ref, g2_ref, vsum_ref = take(7)
    cot, xs, normed, qkv, probs, att, middle, nmid, act, gel, gol, gml, dsc = take(13)
    sums, sums1, b1, outs, gins, keepf, tws, local = take(8)

    images, length, feat = cot.shape
    padded = xs.shape[0] // images
    hidden = act.shape[1]
    hidden_units = hidden // feat
    group = 3 if images % 3 == 0 else 1
    blocks = images // group
    chunk = 256
    half = hidden // 2
    lane = lax.broadcasted_iota(jnp.int32, (padded, 128), 1)
    low_half = lane < HEAD_DIM

    def image_rows(i):
        return pl.ds(pl.multiple_of(i * padded, padded), padded)

    def real_rows(i):
        return pl.ds(pl.multiple_of(i * padded, padded), length)

    def each_block(body, first=0, last=None):
        def step(t, carry):
            rows = pl.ds(pl.multiple_of(t * group * padded, padded), group * padded)
            body(rows, [t * group + k for k in range(group)])
            return carry

        lax.fori_loop(first, blocks if last is None else last, step, 0)

    def row(n):
        return vec_ref[n : n + 1, :]

    def stacked_halves(values):
        zero = jnp.zeros_like(values)
        return jnp.concatenate(
            [jnp.where(low_half, values, zero), jnp.where(low_half, zero, values)], 0
        )

    def merged_halves(values):
        return jnp.where(low_half, values[:padded], values[padded:])

    tok_in = pltpu.make_async_copy(tok_hbm, outs, local.at[0])
    cot_in = pltpu.make_async_copy(cot_hbm, cot, local.at[1])
    out_copy = pltpu.make_async_copy(outs, out_hbm, local.at[2])
    gin_copy = pltpu.make_async_copy(gins, gin_hbm, local.at[3])
    tok_in.start()
    cot_in.start()

    if linked:
        me = lax.axis_index("dp")
        core = lax.axis_index("head")
        layers = dp // PLANE
        layer, place = me // PLANE, me % PLANE
        next_layer = [(layer + r) % layers for r in range(layers)]
        next_place = [(place + r) % PLANE for r in range(PLANE)]
        counter = [0]
        started = []

        def peers(kind):
            if kind == "layer":
                return [(next_layer[r] * PLANE + place, core) for r in range(1, layers)]
            if kind == "cross":
                return [(next_layer[r] * PLANE + place, 1 - core) for r in range(1, layers)]
            if kind == "plane":
                return [(layer * PLANE + next_place[r], core) for r in range(1, PLANE)]
            return [(me, 1 - core)]

        places = {kind: peers(kind) for kind in ("layer", "cross", "plane", "core")}

        def copies_of(ticket):
            kind, pick, first = ticket
            for r, device in enumerate(places[kind], 1):
                src, dst = pick(r)
                yield pltpu.make_async_remote_copy(
                    src_ref=src,
                    dst_ref=dst,
                    send_sem=send.at[first + r - 1],
                    recv_sem=recv.at[first + r - 1],
                    device_id=device,
                    device_id_type=pl.DeviceIdType.MESH,
                )

        def push(kind, pick):
            ticket = (kind, pick, counter[0])
            counter[0] += len(places[kind])
            for copy in copies_of(ticket):
                copy.start()
            started.append(ticket)
            return [ticket]

        def arrive(tickets):
            for ticket in tickets:
                for copy in copies_of(ticket):
                    copy.wait_recv()

        def all_sent():
            for ticket in started:
                for copy in copies_of(ticket):
                    copy.wait_send()
            started.clear()

        barrier = pltpu.get_barrier_semaphore()
        everyone = [device for kind in places.values() for device in kind]
        for device in everyone:
            pl.semaphore_signal(
                barrier, inc=1, device_id=device, device_id_type=pl.DeviceIdType.MESH
            )

        def own_block(u):
            if u < PAIRS:
                parts = [qm_ref[:, n * feat + 128 * u : n * feat + 128 * u + 128] for n in range(3)]
                return jnp.concatenate(parts, 1)
            if u == 3:
                return pm_ref[...]
            if u < 8:
                return f1_ref[:, feat * (u - 4) : feat * (u - 3)]
            return f2_ref[SHARD * (u - 8) : SHARD * (u - 7), :]

        def own_slab(u, other):
            slabs[u + (other - u) * core, place, layer] = jnp.where(
                core == 0, own_block(u), own_block(other)
            ).astype(BF16)

        def vec_push(kind):
            if kind == "layer":
                return push(kind, lambda r: (vslabs.at[place, layer],) * 2)
            return push(kind, lambda r: (vslabs.at[place],) * 2)

        def tot_push(kind, stage):
            part = pl.ds(8 * stage, 8)
            return push(kind, lambda r: (tot_mine.at[part], tot_in.at[3 * stage + r - 1]))

        def tot_sum(stage, count):
            total = tot_mine[8 * stage : 8 * stage + 8]
            for r in range(count):
                total = total + tot_in[3 * stage + r]
            tot_mine[8 * stage + 8 : 8 * stage + 16] = total

        step_units = (
            pl.ds(core, 1), pl.ds(2 + core, 1), pl.ds(4 + 2 * core, 2), pl.ds(8 + 2 * core, 2)
        )
        other = 1 - core
        their_units = (
            pl.ds(other, 1), pl.ds(2 + other, 1), pl.ds(4 + 2 * other, 2), pl.ds(8 + 2 * other, 2)
        )

        def weights_push(step, kind):
            units = step_units[step]
            if kind == "layer":
                return push(kind, lambda r: (slabs.at[units, place, layer],) * 2)
            if kind == "plane":
                return push(kind, lambda r: (slabs.at[units, place],) * 2)
            return push(kind, lambda r: (slabs.at[units],) * 2)

        def two_shards(first, second):
            return jnp.concatenate([first.astype(F32), second.astype(F32)], 0).astype(BF16)

        def assemble(u):
            for q in range(layers):
                for k in range(0, PLANE, 2):
                    both = two_shards(slabs[u, k, q], slabs[u, k + 1, q])
                    first = SHARD * (PLANE * q + k)
                    rows = slice(first, first + 2 * SHARD)
                    if u < PAIRS:
                        wq_ref[rows, feat * u : feat * u + feat] = both
                    elif u == 3:
                        wp_ref[rows, :] = both
                    else:
                        w1_ref[rows, feat * (u - 4) : feat * (u - 3)] = both

        def assemble_w2():
            for q in range(layers):
                for k in range(PLANE):
                    for j in range(0, 4, 2):
                        first = 4 * SHARD * (PLANE * q + k) + SHARD * j
                        w2_ref[first : first + 2 * SHARD, :] = two_shards(
                            slabs[8 + j, k, q], slabs[9 + j, k, q]
                        )

        def spread(values, owner):
            lanes = lax.broadcasted_iota(jnp.int32, (16, 128), 1)
            shift = (SHARD * owner) % 128
            moved = pltpu.roll(values, shift, 1) if shift else values
            block = SHARD * owner // 128
            here = jnp.where(lanes >= shift, moved, 0.0)
            vec_ref[:, 128 * block : 128 * block + 128] += here
            if shift + SHARD > 128:
                rest = jnp.where(lanes < shift, moved, 0.0)
                vec_ref[:, 128 * block + 128 : 128 * block + 256] += rest

        vslabs[place, layer] = jnp.zeros((16, 128), BF16)
        vslabs[place, layer, 0:12, 0:SHARD] = vm_ref[...].astype(BF16)
        own_slab(0, 1)
        kept = jnp.sum(keep_ref[...].astype(F32), 1, keepdims=True)
        width = tot_mine.shape[1]
        source_lane = lax.broadcasted_iota(jnp.int32, (1, width), 1)
        mine = jnp.zeros((1, width), F32)
        for i in range(images):
            mine = mine + jnp.where(source_lane == src_ref[i], kept[i : i + 1], 0.0)
        tot_mine[0:8] = jnp.broadcast_to(mine, (8, width))
        pl.semaphore_wait(barrier, len(everyone))
        vec_go = vec_push("layer")
        go0 = weights_push(0, "layer")
        tot_go = tot_push("layer", 0)
        own_slab(2, 3)
        go1 = weights_push(1, "layer")
        for pair in ((4, 6), (5, 7), (8, 10), (9, 11)):
            own_slab(*pair)
        go2 = weights_push(2, "layer")
        go3 = weights_push(3, "layer")

    for i in range(images):
        tail = slice(padded * (i + 1) - 16, padded * (i + 1))
        xs[tail, :] = jnp.zeros((16, feat), BF16)
        gol[tail, :] = jnp.zeros((16, feat), BF16)
    sums[...] = jnp.zeros_like(sums)
    sums1[...] = jnp.zeros_like(sums1)
    keepf[...] = jnp.zeros_like(keepf)
    keepf[0:images, 0:length] = keep_ref[...].astype(F32)

    def first_norm(_, block):
        for i in block:
            xs[real_rows(i), :] = outs[i]
            unit, _ = normalise(xs[image_rows(i), :].astype(F32))
            middle[image_rows(i), :] = unit

    def first_scale(rows, _):
        normed[rows, :] = (middle[rows, :] * row(0) + row(1)).astype(BF16)

    tok_in.wait()
    each_block(first_norm)

    if linked:
        arrive(vec_go)
        vec_go = vec_push("plane")
        arrive(go0)
        go0 = weights_push(0, "plane")
        arrive(tot_go)
        tot_sum(0, layers - 1)
        tot_go = tot_push("plane", 1)
        arrive(vec_go)
        vec_ref[...] = jnp.zeros_like(vec_ref)
        for owner in range(dp):
            spread(vslabs[owner % PLANE, owner // PLANE].astype(F32), owner)

    for j in range(hidden_units):
        b1[0:1, feat * j : feat * j + feat] = row(8 + j)
    each_block(first_scale)

    if linked:
        arrive(go1)
        arrive(go0)
        go0 = weights_push(0, "core")
        go1 = weights_push(1, "plane")
        arrive(tot_go)
        tot_sum(1, PLANE - 1)
        tot_go = tot_push("core", 2)
        arrive(go2)
        go2 = weights_push(2, "plane")
        arrive(go0)
        assemble(0)
        assemble(1)

    def project(first, last):
        cols = slice(feat * first, feat * last)
        parts = []
        for h in range(first, last):
            part = pl.ds(128 * h, 128)
            parts += [vec_ref[2:3, part], jnp.zeros((1, 128), F32), vec_ref[3:4, part]]
        bias = jnp.concatenate(parts, 1)

        def body(rows, _):
            qkv[rows, cols] = (dot(normed[rows, :], wq_ref[:, cols]) + bias).astype(BF16)

        each_block(body)

    def pair_lanes(h):
        if isinstance(h, int):
            return slice(128 * h, 128 * h + 128)
        return pl.ds(pl.multiple_of(128 * h, 128), 128)

    def head_part(h, n):
        first = feat * h + 128 * n
        if isinstance(h, int):
            return slice(first, first + 128)
        return pl.ds(pl.multiple_of(first, 128), 128)

    def attend(h):
        results = []
        for i in range(images):
            rows = image_rows(i)
            alive = keepf[i : i + 1, 0:padded] > 0
            query = stacked_halves(qkv[rows, head_part(h, 0)] * BF16(SCALE))
            scores = against(query, qkv[rows, head_part(h, 1)])
            scores = jnp.where(alive, scores, -1e9)
            top = jnp.max(scores, -1, keepdims=True)
            raised = jnp.exp(scores - top)
            share = raised * (1.0 / jnp.sum(raised, -1, keepdims=True))
            share = share.astype(BF16)
            mixed = dot(share, qkv[rows, head_part(h, 2)])
            results.append((share, merged_halves(mixed).astype(BF16)))
        out = pair_lanes(h)
        for i, (share, mixed) in enumerate(results):
            probs[h, i] = share
            att[image_rows(i), out] = mixed

    project(0, 2)
    tickets = {}

    def attend_step(h, carry):
        @pl.when(h == 1)
        def _():
            if linked:
                arrive(go1)
                tickets[1] = weights_push(1, "core")
                arrive(go3)
                tickets[3] = weights_push(3, "plane")

        @pl.when(h == 2)
        def _():
            if linked:
                arrive(tickets[1])
                assemble(2)
                assemble(3)
            project(2, 3)

        attend(h)
        return carry

    lax.fori_loop(0, PAIRS, attend_step, 0)

    def second_norm(rows, block):
        middle[rows, :] = xs[rows, :].astype(F32) + (dot(att[rows, :], wp_ref[...]) + row(4))
        for i in block:
            unit, _ = normalise(middle[image_rows(i), :])
            nmid[image_rows(i), :] = (unit * row(5) + row(6)).astype(BF16)

    each_block(second_norm)
    if linked:
        arrive(go2)
        go2 = weights_push(2, "core")

    if linked:
        arrive(tot_go)
        tot_sum(2, 1)
        totals = tot_mine[24:25]
        for i in range(images):
            total = jnp.sum(
                jnp.where(source_lane == src_ref[i], totals, 0.0), 1, keepdims=True
            )
            tws[i : i + 1] = keepf[i : i + 1] * (length / total)
    else:
        tws[...] = jnp.zeros_like(tws)
        tws[0:images, 0:length] = tw_ref[...]
    eye = lax.broadcasted_iota(jnp.int32, (padded, padded), 0) == lax.broadcasted_iota(
        jnp.int32, (padded, padded), 1
    )

    def weigh(_, block):
        for i in block:
            weight_row = tws[pl.ds(i, 1), 0:padded]
            column = jnp.sum(jnp.where(eye, weight_row, 0.0), 1, keepdims=True)
            grad = cot[i].astype(F32) * column[:length]
            gins[i] = grad
            gol[real_rows(i), :] = grad.astype(BF16)

    cot_in.wait()
    each_block(weigh)

    if linked:
        arrive(go2)
        for u in range(4, 8):
            assemble(u)

    def expand(rows, _):
        values = nmid[rows, :]
        for j in range(hidden // chunk):
            cols = slice(chunk * j, chunk * j + chunk)
            active, slope = gelu_parts(dot(values, w1_ref[:, cols]) + b1[0:1, cols])
            act[rows, cols] = active.astype(BF16)
            gel[rows, cols] = slope.astype(BF16)

    each_block(expand, 0, blocks - 1)
    if linked:
        arrive(tickets[3])
        go3 = weights_push(3, "core")
    each_block(expand, blocks - 1, blocks)
    if linked:
        arrive(go3)
        assemble_w2()
        all_sent()

    def hidden_back(rows, _):
        grad = gol[rows, :]
        sums[ROW_FC2] += fold(grad.astype(F32))
        for j in range(hidden // chunk):
            cols = slice(chunk * j, chunk * j + chunk)
            back = against(grad, w2_ref[cols, :]) * gel[rows, cols].astype(F32)
            back = back.astype(BF16)
            gel[rows, cols] = back
            sums1[:, cols] += fold(back.astype(F32))

    each_block(hidden_back)

    if linked:
        slots = ((0, 2), (2, 4), (4, 5), (5, 6))

        first_unit = (8 + 2 * core, 4 + 2 * core, 2 + core, core)
        first_unit_there = (8 + 2 * other, 4 + 2 * other, 2 + other, other)

        def job_slots(job):
            first, last = slots[job]
            return pl.ds(first, last - first)

        def emit(u, grad):
            for owner in range(dp):
                slabs[u, owner % PLANE, owner // PLANE] = grad[
                    SHARD * owner : SHARD * owner + SHARD
                ].astype(BF16)

        def grads_pair(job):
            theirs = their_units[3 - job]
            return push("core", lambda r: (slabs.at[theirs], pair_in.at[job_slots(job)]))

        def grads_plane(job):
            first, last = slots[job]
            for s in range(first, last):
                unit = first_unit[job] + (s - first)
                for k in range(PLANE):
                    for q in range(layers):
                        slabs[unit, k, q] = (
                            slabs[unit, k, q].astype(F32) + pair_in[s, k, q].astype(F32)
                        ).astype(BF16)
            units = step_units[3 - job]
            return push(
                "plane",
                lambda r: (
                    slabs.at[units, next_place[r]],
                    plane_in.at[r - 1, job_slots(job)],
                ),
            )

        def grads_layer(job, both=False):
            first, last = slots[job]
            for s in range(first, last):
                unit = first_unit[job] + (s - first)
                for q in range(layers):
                    total = slabs[unit, place, q].astype(F32)
                    for r in range(PLANE - 1):
                        total = total + plane_in[r, s, q].astype(F32)
                    layer_out[s, q] = total.astype(BF16)
            size = job_slots(job)
            there = lambda r: layer_out.at[size, next_layer[r]]
            copies = push("layer", lambda r: (there(r), layer_in.at[r - 1, size]))
            if both:
                copies += push("cross", lambda r: (there(r), layer_in2.at[pl.ds(r, 1)]))
                copies += push("core", lambda r: (layer_out.at[size, layer], layer_in2.at[pl.ds(0, 1)]))
            return copies

        def grads_share(job, both=False):
            first, last = slots[job]
            for s in range(first, last):
                total = layer_out[s, layer].astype(F32)
                for r in range(layers - 1):
                    total = total + layer_in[r, s].astype(F32)
                share_in[first_unit[job] + (s - first)] = total
            if both:
                total = layer_in2[0].astype(F32)
                for r in range(1, layers):
                    total = total + layer_in2[r].astype(F32)
                share_in[first_unit_there[job]] = total
                return []
            units = step_units[3 - job]
            return push("core", lambda r: (share_in.at[units], share_in.at[units]))

        shares = []

    for n in range(2):
        grad = across(act[:, half * n : half * n + half], gol[...])
        if linked:
            for k in range(dp // 2):
                owner = n * dp // 2 + k
                for j in range(4):
                    first = 4 * SHARD * k + SHARD * j
                    slabs[8 + j, owner % PLANE, owner // PLANE] = grad[
                        first : first + SHARD
                    ].astype(BF16)
        else:
            g2_ref[half * n : half * n + half, :] = grad
    if linked:
        job0 = grads_pair(0)

    def middle_back(rows, block):
        grads = against(gel[rows, :], w1_ref[...])
        for k, i in enumerate(block):
            here = image_rows(i)
            grad = grads[padded * k : padded * k + padded]
            kept_middle = middle[here, :]
            unit, inverse = normalise(kept_middle)
            middle[here, :] = norm_back(grad, unit, inverse, row(5))
            middle[real_rows(i), :] += gins[i]
            gins[i] = kept_middle[:length]
            low = middle[here, :].astype(BF16)
            gml[here, :] = low
            sums[ROW_PROJ] += fold(low.astype(F32))

    each_block(middle_back, 0, 1)
    if linked:
        arrive(job0)
        job0 = grads_plane(0)
    each_block(middle_back, 1, blocks)

    for n in range(2):
        grad = across(nmid[...], gel[:, half * n : half * n + half])
        if linked:
            emit(4 + 2 * n, grad[:, 0:feat])
            emit(5 + 2 * n, grad[:, feat:])
        else:
            g1_ref[:, half * n : half * n + half] = grad
    if linked:
        job1 = grads_pair(1)

    grad = across(att[...], gml[...])
    if linked:
        emit(3, grad)
        arrive(job1)
        job1 = grads_plane(1)
    else:
        gp_ref[...] = grad

    def grad_attended(rows, _):
        att[rows, :] = against(gml[rows, :], wp_ref[...]).astype(BF16)

    each_block(grad_attended)

    def attend_back(h):
        part = pair_lanes(h)
        results = []
        for i in range(images):
            rows = image_rows(i)
            grad = stacked_halves(att[rows, part])
            share = probs[h, i].astype(F32)
            grad_share = against(grad, qkv[rows, head_part(h, 2)])
            inner = jnp.sum(share * grad_share, -1, keepdims=True)
            grad_score = (share * (grad_share - inner)).astype(BF16)
            key = qkv[rows, head_part(h, 1)]
            grad_query = (merged_halves(dot(grad_score, key)) * SCALE).astype(BF16)
            results.append((grad_score, grad_query))
        for i, (grad_score, _) in enumerate(results):
            dsc[i] = grad_score
        moved = []
        for i, (_, grad_query) in enumerate(results):
            rows = image_rows(i)
            query = stacked_halves(qkv[rows, head_part(h, 0)] * BF16(SCALE))
            grad = stacked_halves(att[rows, part])
            grad_key = across(dsc[i], query).astype(BF16)
            grad_value = across(probs[h, i], grad).astype(BF16)
            moved.append((grad_query, grad_key, grad_value))
        for n in range(3):
            for i in range(images):
                qkv[image_rows(i), head_part(h, n)] = moved[i][n]
            sums[n, :, part] = sum(fold(parts[n].astype(F32)) for parts in moved)

    def qkv_grad(first, last):
        cols = slice(feat * first, feat * last)
        grad = across(normed[...], qkv[:, cols])
        for h in range(first, last):
            part = grad[:, feat * (h - first) : feat * (h - first + 1)]
            if linked:
                emit(h, part)
            else:
                gq_ref[:, feat * h : feat * h + feat] = part

    def back_step(t, carry):
        attend_back(PAIRS - 1 - t)

        if t == 0:
            if linked:
                arrive(job0)
                tickets["job0"] = grads_layer(0)
            qkv_grad(2, 3)
            if linked:
                tickets["job2"] = grads_pair(2)

        if t == 1:
            if linked:
                arrive(job1)
                tickets["job1"] = grads_layer(1)
                arrive(tickets["job2"])
                tickets["job2"] = grads_plane(2)

        return carry

    for t in range(PAIRS):
        back_step(t, 0)
    qkv_grad(0, 2)

    def column_sums(out):
        out[...] = jnp.zeros(out.shape, F32)
        for n in range(ROW_FC1):
            out[n : n + 1, :] = jnp.sum(sums[n], 0, keepdims=True)
        for j in range(hidden_units):
            out[ROW_FC1 + j : ROW_FC1 + j + 1, :] = jnp.sum(
                sums1[:, feat * j : feat * j + feat], 0, keepdims=True
            )

    def sums_push(stage, kind):
        return push(kind, lambda r: (vsum.at[stage], vin.at[3 * stage + r - 1]))

    def sums_add(stage, count):
        total = vsum[stage]
        for r in range(count):
            total = total + vin[3 * stage + r]
        vsum[stage + 1] = total

    def contract(rows, block):
        total = dot(act[rows, :], w2_ref[...]) + row(7)
        for k, i in enumerate(block):
            outs[i] = (gins[i] + total[padded * k : padded * k + length]).astype(BF16)

    def input_back(rows, block):
        grads = against(qkv[rows, :], wq_ref[...])
        for k, i in enumerate(block):
            here = image_rows(i)
            unit, inverse = normalise(xs[here, :].astype(F32))
            back = norm_back(grads[padded * k : padded * k + padded], unit, inverse, row(0))
            gins[i] = (middle[here, :] + back)[:length]

    if linked:
        job3 = grads_pair(3)
        column_sums(vsum.at[0])
        vec_go = sums_push(0, "core")
        each_block(contract, 0, 1)
        arrive(job3)
        job3 = grads_plane(3)
        arrive(vec_go)
        sums_add(0, 1)
        vec_go = sums_push(1, "plane")
        arrive(tickets["job0"])
        shares.append(grads_share(0))
        arrive(tickets["job2"])
        job2 = grads_layer(2)
        each_block(contract, 1, blocks)
        out_copy.start()
        arrive(tickets["job1"])
        shares.append(grads_share(1))
        arrive(job3)
        job3 = grads_layer(3, both=True)
        arrive(vec_go)
        sums_add(1, PLANE - 1)
        vec_go = sums_push(2, "layer")
        each_block(input_back)
        gin_copy.start()
        arrive(job2)
        shares.append(grads_share(2))
        arrive(job3)
        shares.append(grads_share(3, both=True))
        arrive(vec_go)
        sums_add(2, layers - 1)
        vsum_ref[...] = vsum[3]
        for copies in shares:
            arrive(copies)
        share_ref[...] = share_in[...]
        all_sent()
    else:
        each_block(contract)
        out_copy.start()
        each_block(input_back)
        gin_copy.start()
        column_sums(vsum_ref)
    out_copy.wait()
    gin_copy.wait()


def layer_call(linked, dp, sources, tokens, cotangent, keep, *rest):
    images, length, feat = tokens.shape
    padded = -(-length // 16) * 16
    hidden = 4 * feat
    rows = images * padded
    vmem = pl.BlockSpec(memory_space=pltpu.VMEM)
    anywhere = pl.BlockSpec(memory_space=pl.ANY)
    smem = pl.BlockSpec(memory_space=pltpu.SMEM)
    shape = jax.ShapeDtypeStruct
    outs = [shape((images, length, feat), BF16), shape((images, length, feat), F32)]
    weights, links = [], []
    params = dict(vmem_limit_bytes=64 * 1024 * 1024)
    if linked:
        layers = dp // PLANE
        width = -(-sources // 128) * 128
        in_specs = [anywhere, anywhere, vmem, smem] + [vmem] * 5
        outs += [shape((UNITS, SHARD, feat), F32), shape((SUM_ROWS, feat), F32)]
        along, beside = layers - 1, PLANE - 1
        copies = 4 * (along + beside + 1) + (along + beside) + (along + beside + 1)
        copies += 4 * (1 + beside + along) + 3 + (along + 1) + (1 + beside + along)
        weights = [
            pltpu.VMEM((feat, PAIRS * feat), BF16),
            pltpu.VMEM((feat, feat), BF16),
            pltpu.VMEM((feat, hidden), BF16),
            pltpu.VMEM((hidden, feat), BF16),
            pltpu.VMEM((16, feat), F32),
        ]
        links = [
            pltpu.VMEM((UNITS, PLANE, layers, SHARD, feat), BF16),
            pltpu.VMEM((PLANE, layers, 16, 128), BF16),
            pltpu.VMEM((32, width), F32),
            pltpu.VMEM((9, 8, width), F32),
            pltpu.VMEM((UNITS // 2, PLANE, layers, SHARD, feat), BF16),
            pltpu.VMEM((beside, UNITS // 2, layers, SHARD, feat), BF16),
            pltpu.VMEM((UNITS // 2, layers, SHARD, feat), BF16),
            pltpu.VMEM((along, UNITS // 2, SHARD, feat), BF16),
            pltpu.VMEM((layers, SHARD, feat), BF16),
            pltpu.VMEM((4, SUM_ROWS, feat), F32),
            pltpu.VMEM((9, SUM_ROWS, feat), F32),
            pltpu.VMEM((UNITS, SHARD, feat), F32),
            pltpu.SemaphoreType.DMA((copies,)),
            pltpu.SemaphoreType.DMA((copies,)),
        ]
        params.update(collective_id=0, has_side_effects=True)
    else:
        in_specs = [anywhere, anywhere] + [vmem] * 7
        outs += [shape(w.shape, F32) for w in rest[1:5]] + [shape((SUM_ROWS, feat), F32)]
    return pl.pallas_call(
        functools.partial(layer_kernel, linked, dp, sources),
        out_shape=outs,
        in_specs=in_specs,
        out_specs=[anywhere, anywhere] + [vmem] * (len(outs) - 2),
        scratch_shapes=weights
        + links
        + [
            pltpu.VMEM((images, length, feat), BF16),
            pltpu.VMEM((rows, feat), BF16),
            pltpu.VMEM((rows, feat), BF16),
            pltpu.VMEM((rows, PAIRS * feat), BF16),
            pltpu.VMEM((PAIRS, images, 2 * padded, padded), BF16),
            pltpu.VMEM((rows, feat), BF16),
            pltpu.VMEM((rows, feat), F32),
            pltpu.VMEM((rows, feat), BF16),
            pltpu.VMEM((rows, hidden), BF16),
            pltpu.VMEM((rows, hidden), BF16),
            pltpu.VMEM((rows, feat), BF16),
            pltpu.VMEM((rows, feat), BF16),
            pltpu.VMEM((images, 2 * padded, padded), BF16),
            pltpu.VMEM((8, 8, feat), F32),
            pltpu.VMEM((8, hidden), F32),
            pltpu.VMEM((8, hidden), F32),
            pltpu.VMEM((images, length, feat), BF16),
            pltpu.VMEM((images, length, feat), F32),
            pltpu.VMEM((16, 256), F32),
            pltpu.VMEM((16, 256), F32),
            pltpu.SemaphoreType.DMA((4,)),
        ],
        compiler_params=pltpu.CompilerParams(**params),
        name="layer",
    )(tokens, cotangent, keep, *rest)


def adamw(master, first, second, gradient, step_rate, weight_decay):
    first_new = 0.9 * first + 0.1 * gradient
    second_new = 0.999 * second + 0.001 * gradient * gradient
    step_size = first_new / (1.0 - 0.9**STEP) / (jnp.sqrt(second_new / (1.0 - 0.999**STEP)) + 1e-08)
    return (first_new, second_new, master - step_rate * (step_size + weight_decay * master))


def norm_grads(products, weighted, gain, bias):
    return (products - bias * weighted) / gain, weighted


def step_kernel(out_tmp, gin_tmp, share_ref, vsum_ref, *refs):
    state, large, outs, held, (came, went) = refs[:15], refs[15:17], refs[17:32], refs[32:34], refs[34:]
    feat = share_ref.shape[2]
    images = out_tmp.shape[0]

    def moves(sources, targets, sems):
        return [
            pltpu.make_async_copy(sources[n].at[i], targets[n].at[i], sems.at[n, i])
            for i in range(images)
            for n in range(2)
        ]

    arrivals = moves((out_tmp, gin_tmp), held, came)
    departures = moves(held, large, went)
    for move in arrivals:
        move.start()

    def update(n, here, gradient):
        new = adamw(
            state[n][here], state[5 + n][here], state[10 + n][here], gradient, step_rates[n], decays[n]
        )
        for k in range(3):
            outs[3 * n + k][here] = new[k]

    def low(values):
        return values.astype(BF16).astype(F32)

    everything = slice(None)
    first_products = jnp.zeros((SHARD, 128), F32)
    first_weighted = jnp.zeros((SHARD, 128), F32)
    for u in range(PAIRS):
        for n in range(3):
            first = n * feat + 128 * u
            cols = slice(first, first + 128)
            grad = share_ref[u, :, 128 * n : 128 * n + 128]
            weight = low(state[0][:, cols])
            first_products += grad * weight
            first_weighted += weight * vsum_ref[n : n + 1, 128 * u : 128 * u + 128]
            update(0, (everything, cols), grad)
    update(1, (everything, everything), share_ref[3])
    second_products = jnp.zeros((SHARD, feat), F32)
    second_weighted = jnp.zeros((SHARD, feat), F32)
    for j in range(4):
        cols = slice(feat * j, feat * j + feat)
        weight = low(state[2][:, cols])
        second_products += share_ref[4 + j] * weight
        second_weighted += weight * vsum_ref[ROW_FC1 + j : ROW_FC1 + j + 1, :]
        update(2, (everything, cols), share_ref[4 + j])
        update(3, (slice(SHARD * j, SHARD * j + SHARD), everything), share_ref[8 + j])

    for arrival, departure in zip(arrivals, departures):
        arrival.wait()
        departure.start()

    me = lax.axis_index("dp")
    sums = vsum_ref[...]
    lanes = lax.broadcasted_iota(jnp.int32, (SUM_ROWS, 128), 1)
    mine = jnp.zeros((SUM_ROWS, 128), F32)
    for owner in range(16):
        shift = (SHARD * owner) % 128
        block = SHARD * owner // 128
        part = sums[:, 128 * block : 128 * block + 128]
        part = pltpu.roll(part, 128 - shift, 1) if shift else part
        if shift + SHARD > 128:
            rest = pltpu.roll(sums[:, 128 * block + 128 : 128 * block + 256], 128 - shift, 1)
            part = jnp.where(lanes < 128 - shift, part, rest)
        mine = jnp.where(me == owner, part, mine)
    mine = mine[:, 0:SHARD]
    eye = lax.broadcasted_iota(jnp.int32, (SHARD, SHARD), 0) == lax.broadcasted_iota(
        jnp.int32, (SHARD, SHARD), 1
    )

    def as_row(values):
        column = jnp.sum(values, 1, keepdims=True)
        return jnp.sum(jnp.where(eye, column, 0.0), 0, keepdims=True)

    vec = low(state[4][...])
    gain_first, shift_first = norm_grads(
        as_row(first_products), as_row(first_weighted), vec[0:1], vec[1:2]
    )
    gain_second, shift_second = norm_grads(
        as_row(second_products), as_row(second_weighted), vec[5:6], vec[6:7]
    )
    grads = [gain_first, shift_first, mine[0:1], mine[2:3], mine[ROW_PROJ : ROW_PROJ + 1]]
    grads += [gain_second, shift_second, mine[ROW_FC2 : ROW_FC2 + 1]]
    grads += [mine[ROW_FC1 + j : ROW_FC1 + j + 1] for j in range(4)]
    for n, grad in enumerate(grads):
        update(4, (slice(n, n + 1), everything), grad)
    for move in departures:
        move.wait()


def step_call(layer_out, input_grad, share, vsum, states):
    vmem = pl.BlockSpec(memory_space=pltpu.VMEM)
    anywhere = pl.BlockSpec(memory_space=pl.ANY)
    shape = jax.ShapeDtypeStruct
    large = [shape(a.shape, a.dtype) for a in (layer_out, input_grad)]
    return pl.pallas_call(
        step_kernel,
        out_shape=large + [shape(states[n].shape, F32) for n in range(5) for _ in range(3)],
        in_specs=[anywhere] * 2 + [vmem] * 17,
        out_specs=[anywhere] * 2 + [vmem] * 15,
        scratch_shapes=[pltpu.VMEM(a.shape, a.dtype) for a in (layer_out, input_grad)]
        + [pltpu.SemaphoreType.DMA((2, layer_out.shape[0]))] * 2,
        compiler_params=pltpu.CompilerParams(vmem_limit_bytes=64 * 1024 * 1024),
        name="step",
    )(layer_out, input_grad, share, vsum, *states)


def by_pair(weight):
    rows, cols = weight.shape
    return weight.reshape(rows, 3, PAIRS, 128).transpose(0, 2, 1, 3).reshape(rows, cols)


def from_pairs(grad):
    rows, cols = grad.shape
    return grad.reshape(rows, PAIRS, 3, 128).transpose(0, 2, 1, 3).reshape(rows, cols)


def on_device(tokens, cotangent, keep_mask, source, *states):
    masters = states[:5]
    dp = lax.axis_size("dp")
    images, length, feat = tokens.shape
    sources = images * lax.axis_size("head") * dp // 3
    if dp == 16:
        layer_out, input_grad, share, vsum = layer_call(
            True, dp, sources, tokens, cotangent, keep_mask, source, *masters
        )
        return tuple(step_call(layer_out, input_grad, share, vsum, states))
    gather = functools.partial(lax.all_gather, axis_name="dp", tiled=True)
    low = [master.astype(BF16) for master in masters]
    w_qkv, w_proj, w_fc1, w_fc2 = (gather(w, axis=0) for w in low[:4])
    vectors = gather(low[4], axis=1).astype(F32)
    live_mask = keep_mask.astype(F32)
    kept_rows = jnp.sum(live_mask, 1)
    onehot = (source[:, None] == jnp.arange(sources, dtype=jnp.int32)[None, :]).astype(F32)
    totals = lax.psum(jnp.sum(onehot * kept_rows[:, None], 0), ("dp", "head"))
    image_total = jnp.sum(onehot * totals[None, :], 1)
    token_weight = live_mask * (length / image_total)[:, None]
    layer_out, input_grad, gq, gp, g1, g2, vsum = layer_call(
        False, dp, sources, tokens, cotangent, keep_mask,
        token_weight, by_pair(w_qkv), w_proj, w_fc1, w_fc2, vectors,
    )
    shares = [
        lax.psum_scatter(
            lax.psum(g.astype(BF16), "head").astype(F32), "dp", scatter_dimension=0, tiled=True
        )
        for g in (from_pairs(gq), gp, g1, g2)
    ]
    vsum = lax.psum(vsum, ("dp", "head"))
    low = [w.astype(F32) for w in low]
    own = masters[4].shape[1]
    mine = lax.dynamic_slice_in_dim(vsum, lax.axis_index("dp") * own, own, 1)
    norms = []
    for share, weight, behind, n in (
        (shares[0], low[0], vsum[:3], 0),
        (shares[2], low[2], vsum[ROW_FC1 : ROW_FC1 + 4], 5),
    ):
        products = jnp.sum(share * weight, 1)
        weighted = jnp.sum(weight * behind.reshape(1, -1), 1)
        norms.append(norm_grads(products, weighted, low[4][n], low[4][n + 1]))
    rows = [*norms[0], mine[0], mine[2], mine[ROW_PROJ], *norms[1], mine[ROW_FC2]]
    shares.append(jnp.stack(rows + [mine[ROW_FC1 + j] for j in range(4)]))
    new = []
    for n in range(5):
        new.extend(
            adamw(masters[n], states[5 + n], states[10 + n], shares[n], step_rates[n], decays[n])
        )
    return (layer_out, input_grad, *new)


def solution(mesh):
    split = P(("dp", "head"), None, None)
    rows, cols = P("dp", None), P(None, "dp")
    weights = (rows, rows, rows, rows, cols)
    return jax.shard_map(
        on_device,
        mesh=mesh,
        in_specs=(split, split, P(("dp", "head"), None), P(("dp", "head"))) + weights * 3,
        out_specs=(split, split) + (rows,) * 12 + (cols,) * 3,
        check_vma=False,
    )
```

profile of v0, /device:TPU:0, one launch (start us, length us, event | category | flops | bytes accessed | tf_op | source)
XLA Modules:
  0.0 94.0 jit_solution(5885199002482458729)
XLA Ops:
  0.7 86.4 %layer.1 = (bf16[9,198,384]{2,1,0:T(8,128)(2,1)}, f32[9,198,384]{2,1,0:T(8,128)}, f32[12,24,384]{2,1,0:T(8,128)}, f32[16,384]{1,0:T(8,128)}) custom-call(bf16[9,198,384]{2,1,0:T(8,128)(2,1)} %refs_0_.2, bf16[9,198,384]{2,1,0:T(8,128)(2,1)} %refs_1_.2, s32[9,198]{1,0:T(8,128)} %refs_2_.2, s32[9]{0:T(128)} %refs_3_.2, f32[24,1152]{1,0:T(8,128)} %refs_0_.3, ...), custom_call_target="tpu_custom_call" | custom-call | tf_op jit(solution)/shard_map/layer/pallas_call | solution.py:810
  87.1 6.8 %step.1 = (bf16[9,198,384]{2,1,0:T(8,128)(2,1)}, f32[9,198,384]{2,1,0:T(8,128)}, f32[24,1152]{1,0:T(8,128)}, f32[24,1152]{1,0:T(8,128)}, f32[24,1152]{1,0:T(8,12...) custom-call(bf16[9,198,384]{2,1,0:T(8,128)(2,1)} %get-tuple-element., ...), custom_call_target="tpu_custom_call" | custom-call | tf_op jit(solution)/shard_map/step/pallas_call | solution.py:953
where the time goes:
time: 94.2 us; the launch traced here: 94 us
  Pallas kernels  93.2 us (99%)
    pallas_call x1, Pallas kernels, layer_call(): pl.pallas_call(functools.partial(layer_kernel, linked, dp, sources), out_...  86.4 us
    pallas_call x1, Pallas kernels, step_call(): pl.pallas_call(step_kernel, out_shape=large + [shape(states[n].shape, F32...  6.77 us

commit v1 on v0

--- a/solution.py
+++ b/solution.py
@@ -243,12 +243,15 @@
         def two_shards(first, second):
             return jnp.concatenate([first.astype(F32), second.astype(F32)], 0).astype(BF16)
 
+        def each_layer(body):
+            lax.fori_loop(0, layers, lambda q, c: (body(q), c)[1], 0)
+
         def assemble(u):
-            for q in range(layers):
+            def body(q):
                 for k in range(0, PLANE, 2):
                     both = two_shards(slabs[u, k, q], slabs[u, k + 1, q])
-                    first = SHARD * (PLANE * q + k)
-                    rows = slice(first, first + 2 * SHARD)
+                    first = pl.multiple_of(SHARD * PLANE * q + SHARD * k, 16)
+                    rows = pl.ds(first, 2 * SHARD)
                     if u < PAIRS:
                         wq_ref[rows, feat * u : feat * u + feat] = both
                     elif u == 3:
@@ -256,14 +259,18 @@
                     else:
                         w1_ref[rows, feat * (u - 4) : feat * (u - 3)] = both
 
+            each_layer(body)
+
         def assemble_w2():
-            for q in range(layers):
+            def body(q):
                 for k in range(PLANE):
                     for j in range(0, 4, 2):
-                        first = 4 * SHARD * (PLANE * q + k) + SHARD * j
-                        w2_ref[first : first + 2 * SHARD, :] = two_shards(
+                        first = pl.multiple_of(4 * SHARD * (PLANE * q + k) + SHARD * j, 16)
+                        w2_ref[pl.ds(first, 2 * SHARD), :] = two_shards(
                             slabs[8 + j, k, q], slabs[9 + j, k, q]
                         )
+
+            each_layer(body)
 
         def spread(values, owner):
             lanes = lax.broadcasted_iota(jnp.int32, (16, 128), 1)
@@ -514,11 +521,14 @@
             first, last = slots[job]
             for s in range(first, last):
                 unit = first_unit[job] + (s - first)
-                for k in range(PLANE):
-                    for q in range(layers):
+
+                def body(q):
+                    for k in range(PLANE):
                         slabs[unit, k, q] = (
                             slabs[unit, k, q].astype(F32) + pair_in[s, k, q].astype(F32)
                         ).astype(BF16)
+
+                each_layer(body)
             units = step_units[3 - job]
             return push(
                 "plane",
@@ -853,22 +863,66 @@
     return (products - bias * weighted) / gain, weighted
 
 
-def step_kernel(out_tmp, gin_tmp, share_ref, vsum_ref, *refs):
-    state, large, outs, held, (came, went) = refs[:15], refs[15:17], refs[17:32], refs[32:34], refs[34:]
+def step_kernel(*refs):
+    refs = list(refs)
+
+    def take(count):
+        taken = refs[:count]
+        del refs[:count]
+        return taken
+
+    large_in, small_in, large_out, state_out = take(2), take(17), take(2), take(15)
+    large, small, outs = take(2), take(17), take(15)
+    came, went, small_came, small_went = take(4)
+    share_ref, vsum_ref, *state = small
     feat = share_ref.shape[2]
-    images = out_tmp.shape[0]
+    images = large[0].shape[0]
+    parts = came.shape[1]
+    size = images // parts
 
     def moves(sources, targets, sems):
         return [
-            pltpu.make_async_copy(sources[n].at[i], targets[n].at[i], sems.at[n, i])
-            for i in range(images)
+            pltpu.make_async_copy(
+                sources[n].at[pl.ds(size * i, size)], targets[n].at[pl.ds(size * i, size)], sems.at[n, i]
+            )
+            for i in range(parts)
             for n in range(2)
         ]
 
-    arrivals = moves((out_tmp, gin_tmp), held, came)
-    departures = moves(held, large, went)
-    for move in arrivals:
+    def copies(sources, targets, sems):
+        return [
+            pltpu.make_async_copy(src, dst, sems.at[n])
+            for n, (src, dst) in enumerate(zip(sources, targets))
+        ]
+
+    arrivals, departures = moves(large_in, large, came), moves(large, large_out, went)
+    small_arrivals = copies(small_in, small, small_came)
+    small_departures = copies(outs, state_out, small_went)
+
+    def fetch(n):
+        return [small_arrivals[2 + 5 * k + n] for k in range(3)]
+
+    order = [small_arrivals[0], *fetch(0), *fetch(2), *fetch(3)]
+    order += [small_arrivals[1], *fetch(1), *fetch(4)]
+    for move in order[:4] + arrivals + order[4:]:
         move.start()
+
+    def ready(n):
+        for move in fetch(n):
+            move.wait()
+
+    def store(n):
+        for k in range(3):
+            small_departures[3 * n + k].start()
+
+    def pass_on(count):
+        for _ in range(count):
+            arrivals[0].wait()
+            departures[0].start()
+            del arrivals[0]
+            left.append(departures.pop(0))
+
+    left = []
 
     def update(n, here, gradient):
         new = adamw(
@@ -881,8 +935,11 @@
         return values.astype(BF16).astype(F32)
 
     everything = slice(None)
+    small_arrivals[0].wait()
+    small_arrivals[1].wait()
     first_products = jnp.zeros((SHARD, 128), F32)
     first_weighted = jnp.zeros((SHARD, 128), F32)
+    ready(0)
     for u in range(PAIRS):
         for n in range(3):
             first = n * feat + 128 * u
@@ -892,20 +949,28 @@
             first_products += grad * weight
             first_weighted += weight * vsum_ref[n : n + 1, 128 * u : 128 * u + 128]
             update(0, (everything, cols), grad)
-    update(1, (everything, everything), share_ref[3])
+    store(0)
+    pass_on(2)
     second_products = jnp.zeros((SHARD, feat), F32)
     second_weighted = jnp.zeros((SHARD, feat), F32)
+    ready(2)
     for j in range(4):
         cols = slice(feat * j, feat * j + feat)
         weight = low(state[2][:, cols])
         second_products += share_ref[4 + j] * weight
         second_weighted += weight * vsum_ref[ROW_FC1 + j : ROW_FC1 + j + 1, :]
         update(2, (everything, cols), share_ref[4 + j])
+    store(2)
+    pass_on(2)
+    ready(3)
+    for j in range(4):
         update(3, (slice(SHARD * j, SHARD * j + SHARD), everything), share_ref[8 + j])
-
-    for arrival, departure in zip(arrivals, departures):
-        arrival.wait()
-        departure.start()
+    store(3)
+    ready(1)
+    update(1, (everything, everything), share_ref[3])
+    store(1)
+    ready(4)
+    pass_on(len(arrivals))
 
     me = lax.axis_index("dp")
     sums = vsum_ref[...]
@@ -941,25 +1006,29 @@
     grads += [mine[ROW_FC1 + j : ROW_FC1 + j + 1] for j in range(4)]
     for n, grad in enumerate(grads):
         update(4, (slice(n, n + 1), everything), grad)
-    for move in departures:
+    store(4)
+    for move in left + small_departures:
         move.wait()
 
 
 def step_call(layer_out, input_grad, share, vsum, states):
-    vmem = pl.BlockSpec(memory_space=pltpu.VMEM)
     anywhere = pl.BlockSpec(memory_space=pl.ANY)
     shape = jax.ShapeDtypeStruct
     large = [shape(a.shape, a.dtype) for a in (layer_out, input_grad)]
+    new = [shape(states[n].shape, F32) for n in range(5) for _ in range(3)]
+    operands = (layer_out, input_grad, share, vsum, *states)
+    parts = 3 if layer_out.shape[0] % 3 == 0 else 1
+    dma = pltpu.SemaphoreType.DMA
     return pl.pallas_call(
         step_kernel,
-        out_shape=large + [shape(states[n].shape, F32) for n in range(5) for _ in range(3)],
-        in_specs=[anywhere] * 2 + [vmem] * 17,
-        out_specs=[anywhere] * 2 + [vmem] * 15,
-        scratch_shapes=[pltpu.VMEM(a.shape, a.dtype) for a in (layer_out, input_grad)]
-        + [pltpu.SemaphoreType.DMA((2, layer_out.shape[0]))] * 2,
+        out_shape=large + new,
+        in_specs=[anywhere] * len(operands),
+        out_specs=[anywhere] * 17,
+        scratch_shapes=[pltpu.VMEM(a.shape, a.dtype) for a in (*operands, *new)]
+        + [dma((2, parts)), dma((2, parts)), dma((17,)), dma((15,))],
         compiler_params=pltpu.CompilerParams(vmem_limit_bytes=64 * 1024 * 1024),
         name="step",
-    )(layer_out, input_grad, share, vsum, *states)
+    )(*operands)
 
 
 def by_pair(weight):

time: 94.2 us -> 92.7 us (0.984)
  Pallas kernels: 93.2 us -> 91.7 us
    pallas_call x1, Pallas kernels: 6.77 us -> 4.98 us  [step_call(): pl.pallas_call(step_kernel, out_shape=large + new, in_specs=[anywhere] *...]
where the time goes in v1:
time: 92.7 us; the launch traced here: 92.5 us
  Pallas kernels  91.7 us (99%)
    pallas_call x1, Pallas kernels, layer_call(): pl.pallas_call(functools.partial(layer_kernel, linked, dp, sources), out_...  86.7 us
    pallas_call x1, Pallas kernels, step_call(): pl.pallas_call(step_kernel, out_shape=large + new, in_specs=[anywhere] *...  4.98 us

profile of v1, /device:TPU:0, one launch (start us, length us, event | category | flops | bytes accessed | tf_op | source)
XLA Modules:
  0.0 92.5 jit_solution(16196819336515106176)
XLA Ops:
  0.7 86.7 %layer.1 = (bf16[9,198,384]{2,1,0:T(8,128)(2,1)}, f32[9,198,384]{2,1,0:T(8,128)}, f32[12,24,384]{2,1,0:T(8,128)}, f32[16,384]{1,0:T(8,128)}) custom-call(bf16[9,198,384]{2,1,0:T(8,128)(2,1)} %refs_0_.1, bf16[9,198,384]{2,1,0:T(8,128)(2,1)} %refs_1_.1, s32[9,198]{1,0:T(8,128)} %refs_2_.1, s32[9]{0:T(128)} %refs_3_.1, f32[24,1152]{1,0:T(8,128)} %refs_4_.3, ...), custom_call_target="tpu_custom_call" | custom-call | tf_op jit(solution)/shard_map/layer/pallas_call | solution.py:820
  87.3 5.0 %step.1 = (bf16[9,198,384]{2,1,0:T(8,128)(2,1)}, f32[9,198,384]{2,1,0:T(8,128)}, f32[24,1152]{1,0:T(8,128)}, f32[24,1152]{1,0:T(8,128)}, f32[24,1152]{1,0:T(8,12...) custom-call(bf16[9,198,384]{2,1,0:T(8,128)(2,1)} %get-tuple-element., ...), custom_call_target="tpu_custom_call" | custom-call | tf_op jit(solution)/shard_map/step/pallas_call | solution.py:1022

commit v2 on v1

--- a/solution.py
+++ b/solution.py
@@ -83,7 +83,7 @@
         out_hbm, gin_hbm, share_ref, vsum_ref = take(4)
         wq_ref, wp_ref, w1_ref, w2_ref, vec_ref = take(5)
         slabs, vslabs, tot_mine, tot_in, pair_in, plane_in, layer_out, layer_in, layer_in2 = take(9)
-        vsum, vin, share_in, send, recv = take(5)
+        vsum, vin, late, late_in, share_in, send, recv = take(7)
     else:
         tw_ref, wq_ref, wp_ref, w1_ref, w2_ref, vec_ref = take(6)
         out_hbm, gin_hbm, gq_ref, gp_ref, g1_ref, g2_ref, vsum_ref = take(7)
@@ -669,30 +669,6 @@
             else:
                 gq_ref[:, feat * h : feat * h + feat] = part
 
-    def back_step(t, carry):
-        attend_back(PAIRS - 1 - t)
-
-        if t == 0:
-            if linked:
-                arrive(job0)
-                tickets["job0"] = grads_layer(0)
-            qkv_grad(2, 3)
-            if linked:
-                tickets["job2"] = grads_pair(2)
-
-        if t == 1:
-            if linked:
-                arrive(job1)
-                tickets["job1"] = grads_layer(1)
-                arrive(tickets["job2"])
-                tickets["job2"] = grads_plane(2)
-
-        return carry
-
-    for t in range(PAIRS):
-        back_step(t, 0)
-    qkv_grad(0, 2)
-
     def column_sums(out):
         out[...] = jnp.zeros(out.shape, F32)
         for n in range(ROW_FC1):
@@ -705,11 +681,48 @@
     def sums_push(stage, kind):
         return push(kind, lambda r: (vsum.at[stage], vin.at[3 * stage + r - 1]))
 
-    def sums_add(stage, count):
-        total = vsum[stage]
+    def late_push(stage, kind):
+        return push(kind, lambda r: (late.at[stage], late_in.at[3 * stage + r - 1]))
+
+    def sums_add(stage, count, own, came):
+        total = own[stage]
         for r in range(count):
-            total = total + vin[3 * stage + r]
-        vsum[stage + 1] = total
+            total = total + came[3 * stage + r]
+        own[stage + 1] = total
+
+    def back_step(t, carry):
+        attend_back(PAIRS - 1 - t)
+
+        if t == 0:
+            if linked:
+                arrive(job0)
+                tickets["job0"] = grads_layer(0)
+            qkv_grad(2, 3)
+            if linked:
+                tickets["job2"] = grads_pair(2)
+
+        if t == 1:
+            if linked:
+                arrive(job1)
+                tickets["job1"] = grads_layer(1)
+                arrive(tickets["job2"])
+                tickets["job2"] = grads_plane(2)
+                column_sums(vsum.at[0])
+                tickets["vec"] = sums_push(0, "core")
+
+        return carry
+
+    for t in range(PAIRS):
+        back_step(t, 0)
+    if linked:
+        arrive(tickets["vec"])
+        sums_add(0, 1, vsum, vin)
+        vec_go = sums_push(1, "plane")
+        late[0] = jnp.zeros((8, 128), F32)
+        for n in range(3):
+            late[0, n : n + 1, :] = jnp.sum(sums[n, :, 0:128], 0, keepdims=True)
+        late_go = late_push(0, "core")
+    qkv_grad(0, 2)
 
     def contract(rows, block):
         total = dot(act[rows, :], w2_ref[...]) + row(7)
@@ -726,35 +739,40 @@
 
     if linked:
         job3 = grads_pair(3)
-        column_sums(vsum.at[0])
-        vec_go = sums_push(0, "core")
+        arrive(late_go)
+        sums_add(0, 1, late, late_in)
         each_block(contract, 0, 1)
         arrive(job3)
         job3 = grads_plane(3)
-        arrive(vec_go)
-        sums_add(0, 1)
-        vec_go = sums_push(1, "plane")
+        late_go = late_push(1, "plane")
+        arrive(tickets["job2"])
+        job2 = grads_layer(2)
         arrive(tickets["job0"])
         shares.append(grads_share(0))
-        arrive(tickets["job2"])
-        job2 = grads_layer(2)
+        arrive(vec_go)
+        sums_add(1, PLANE - 1, vsum, vin)
+        vec_go = sums_push(2, "layer")
         each_block(contract, 1, blocks)
         out_copy.start()
         arrive(tickets["job1"])
         shares.append(grads_share(1))
+        each_block(input_back, 0, 1)
         arrive(job3)
         job3 = grads_layer(3, both=True)
-        arrive(vec_go)
-        sums_add(1, PLANE - 1)
-        vec_go = sums_push(2, "layer")
-        each_block(input_back)
+        arrive(late_go)
+        sums_add(1, PLANE - 1, late, late_in)
+        late_go = late_push(2, "layer")
+        each_block(input_back, 1, blocks)
         gin_copy.start()
         arrive(job2)
         shares.append(grads_share(2))
+        arrive(vec_go)
+        sums_add(2, layers - 1, vsum, vin)
+        arrive(late_go)
+        sums_add(2, layers - 1, late, late_in)
+        vsum[3, 0:3, 0:128] = late[3, 0:3, :]
         arrive(job3)
         shares.append(grads_share(3, both=True))
-        arrive(vec_go)
-        sums_add(2, layers - 1)
         vsum_ref[...] = vsum[3]
         for copies in shares:
             arrive(copies)
@@ -789,7 +807,7 @@
         outs += [shape((UNITS, SHARD, feat), F32), shape((SUM_ROWS, feat), F32)]
         along, beside = layers - 1, PLANE - 1
         copies = 4 * (along + beside + 1) + (along + beside) + (along + beside + 1)
-        copies += 4 * (1 + beside + along) + 3 + (along + 1) + (1 + beside + along)
+        copies += 4 * (1 + beside + along) + 3 + (along + 1) + 2 * (1 + beside + along)
         weights = [
             pltpu.VMEM((feat, PAIRS * feat), BF16),
             pltpu.VMEM((feat, feat), BF16),
@@ -809,6 +827,8 @@
             pltpu.VMEM((layers, SHARD, feat), BF16),
             pltpu.VMEM((4, SUM_ROWS, feat), F32),
             pltpu.VMEM((9, SUM_ROWS, feat), F32),
+            pltpu.VMEM((4, 8, 128), F32),
+            pltpu.VMEM((9, 8, 128), F32),
             pltpu.VMEM((UNITS, SHARD, feat), F32),
             pltpu.SemaphoreType.DMA((copies,)),
             pltpu.SemaphoreType.DMA((copies,)),

time: 92.7 us -> 92 us (level)
  no operation moved by 1% of the time
where the time goes in v2:
time: 92 us; the launch traced here: 91.8 us
  Pallas kernels  91 us (99%)
    pallas_call x1, Pallas kernels, layer_call(): pl.pallas_call(functools.partial(layer_kernel, linked, dp, sources), out_...  86 us
    pallas_call x1, Pallas kernels, step_call(): pl.pallas_call(step_kernel, out_shape=large + new, in_specs=[anywhere] *...  4.98 us

profile of v2, /device:TPU:0, one launch (start us, length us, event | category | flops | bytes accessed | tf_op | source)
XLA Modules:
  0.0 91.8 jit_solution(8872884473482006341)
XLA Ops:
  0.7 86.0 %layer.1 = (bf16[9,198,384]{2,1,0:T(8,128)(2,1)}, f32[9,198,384]{2,1,0:T(8,128)}, f32[12,24,384]{2,1,0:T(8,128)}, f32[16,384]{1,0:T(8,128)}) custom-call(bf16[9,198,384]{2,1,0:T(8,128)(2,1)} %refs_0_.1, bf16[9,198,384]{2,1,0:T(8,128)(2,1)} %refs_1_.1, s32[9,198]{1,0:T(8,128)} %refs_2_.1, s32[9]{0:T(128)} %refs_3_.1, f32[24,1152]{1,0:T(8,128)} %refs_4_.3, ...), custom_call_target="tpu_custom_call" | custom-call | tf_op jit(solution)/shard_map/layer/pallas_call | solution.py:840
  86.7 5.0 %step.1 = (bf16[9,198,384]{2,1,0:T(8,128)(2,1)}, f32[9,198,384]{2,1,0:T(8,128)}, f32[24,1152]{1,0:T(8,128)}, f32[24,1152]{1,0:T(8,128)}, f32[24,1152]{1,0:T(8,12...) custom-call(bf16[9,198,384]{2,1,0:T(8,128)(2,1)} %get-tuple-element., ...), custom_call_target="tpu_custom_call" | custom-call | tf_op jit(solution)/shard_map/step/pallas_call | solution.py:1042

commit v3 on v2

--- a/solution.py
+++ b/solution.py
@@ -481,9 +481,9 @@
         go3 = weights_push(3, "core")
     each_block(expand, blocks - 1, blocks)
     if linked:
+        all_sent()
         arrive(go3)
         assemble_w2()
-        all_sent()
 
     def hidden_back(rows, _):
         grad = gol[rows, :]
@@ -771,13 +771,13 @@
         arrive(late_go)
         sums_add(2, layers - 1, late, late_in)
         vsum[3, 0:3, 0:128] = late[3, 0:3, :]
+        all_sent()
         arrive(job3)
         shares.append(grads_share(3, both=True))
         vsum_ref[...] = vsum[3]
         for copies in shares:
             arrive(copies)
         share_ref[...] = share_in[...]
-        all_sent()
     else:
         each_block(contract)
         out_copy.start()
@@ -924,7 +924,7 @@
 
     order = [small_arrivals[0], *fetch(0), *fetch(2), *fetch(3)]
     order += [small_arrivals[1], *fetch(1), *fetch(4)]
-    for move in order[:4] + arrivals + order[4:]:
+    for move in arrivals[:2] + order[:4] + arrivals[2:] + order[4:]:
         move.start()
 
     def ready(n):
@@ -959,6 +959,7 @@
     small_arrivals[1].wait()
     first_products = jnp.zeros((SHARD, 128), F32)
     first_weighted = jnp.zeros((SHARD, 128), F32)
+    pass_on(2)
     ready(0)
     for u in range(PAIRS):
         for n in range(3):

time: 92 us -> 91.7 us (level)
  no operation moved by 1% of the time
where the time goes in v3:
time: 91.7 us; the launch traced here: 91.6 us
  Pallas kernels  90.7 us (99%)
    pallas_call x1, Pallas kernels, layer_call(): pl.pallas_call(functools.partial(layer_kernel, linked, dp, sources), out_...  86 us
    pallas_call x1, Pallas kernels, step_call(): pl.pallas_call(step_kernel, out_shape=large + new, in_specs=[anywhere] *...  4.66 us

profile of v3, /device:TPU:0, one launch (start us, length us, event | category | flops | bytes accessed | tf_op | source)
XLA Modules:
  0.0 91.6 jit_solution(18218442041661131320)
XLA Ops:
  0.7 86.0 %layer.1 = (bf16[9,198,384]{2,1,0:T(8,128)(2,1)}, f32[9,198,384]{2,1,0:T(8,128)}, f32[12,24,384]{2,1,0:T(8,128)}, f32[16,384]{1,0:T(8,128)}) custom-call(bf16[9,198,384]{2,1,0:T(8,128)(2,1)} %refs_0_.1, bf16[9,198,384]{2,1,0:T(8,128)(2,1)} %refs_1_.1, s32[9,198]{1,0:T(8,128)} %refs_2_.1, s32[9]{0:T(128)} %refs_3_.1, f32[24,1152]{1,0:T(8,128)} %refs_4_.3, ...), custom_call_target="tpu_custom_call" | custom-call | tf_op jit(solution)/shard_map/layer/pallas_call | solution.py:840
  86.7 4.7 %step.1 = (bf16[9,198,384]{2,1,0:T(8,128)(2,1)}, f32[9,198,384]{2,1,0:T(8,128)}, f32[24,1152]{1,0:T(8,128)}, f32[24,1152]{1,0:T(8,128)}, f32[24,1152]{1,0:T(8,12...) custom-call(bf16[9,198,384]{2,1,0:T(8,128)(2,1)} %get-tuple-element., ...), custom_call_target="tpu_custom_call" | custom-call | tf_op jit(solution)/shard_map/step/pallas_call | solution.py:1043
